TPU v7x, 32 devices: a whole 2x2x4 slice. The times are simulated.
32 devices in a mesh: groups: 2 (over x), dp: 16 (over z, y, core).
Axes of the slice: x: 2, y: 2, z: 4, core: 2. Of those that a mesh axis runs over, the one named last changes fastest.
Arguments:
- acts: bfloat16 [4096, 8192], P(('groups', 'dp')), parts along dimension 0, may hold values from -6 to 6
- grads_out: bfloat16 [4096, 8192], P(('groups', 'dp')), parts along dimension 0, may hold values from -0.3984375 to 0.3984375
- tenant_ids: int32 [4096, 1], P(('groups', 'dp')), parts along dimension 0, may hold values from 0 to 7; in each aligned block of 128 rows (0 to 127, 128 to 255, ...) at most 32 rows name the same one
- owner: int32 [16], P('groups'), parts along dimension 0, may hold values from 0 to 7, each once
- a_half: float32 [32, 4096, 64], P(('groups', 'dp')), parts along dimension 0, may hold values from -0.0625 to 0.0625
- b_half: float32 [32, 64, 4096], P(('groups', 'dp')), parts along dimension 0, may hold values from -0.75 to 0.75
Outputs:
- input_grad: float32 [4096, 8192], P(('groups', 'dp')), parts along dimension 0
- grad_a: float32 [32, 4096, 64], P(('groups', 'dp')), parts along dimension 0
- grad_b: float32 [32, 64, 4096], P(('groups', 'dp')), parts along dimension 0
There are 2 independent parts, one for each index of `groups`. A program takes and returns all parts, laid end to end along the dimension named above; each array names one. Nothing has to cross between parts.
Inputs may be any that keep to these rules, and one draw needn't show every extreme that they name: `tenant_ids`: one device's rows name each tenant at most 32 times. `owner`: each slot holds exactly one tenant.
All inputs are finite; a program needn't handle non-finite values.
Results may differ from a plain program's by a relative error of at most 0.0003.
Values may be sent and summed in bfloat16 or wider, within the bound.
A program may use at most 128 MiB of HBM per device.

v0:
```python
import jax
import jax.numpy as jnp
from jax import lax
from jax.sharding import PartitionSpec as P


def from_partner(value, axis, stride):
    mask = 2**stride
    pairs = [(source, source ^ mask) for source in range(lax.axis_size(axis))]
    return lax.ppermute(value, axis, pairs)


def exact(left, right):
    return jnp.dot(left, right, precision=lax.Precision.HIGHEST, preferred_element_type=jnp.float32)


def placement(dest, slots):
    return (jnp.arange(slots, dtype=jnp.int32)[:, None] == dest[None, :]).astype(jnp.bfloat16)


def body(acts, grads_out, tenant_ids, owner, a_half, b_half):
    row_count, width = acts.shape
    group_size = lax.axis_size("dp")
    tenants = owner.shape[0]
    capacity = 4 * row_count // group_size
    half_width = width // 2
    first_half = lax.axis_index("dp") % 2 == 0
    onehot = (tenant_ids[:, 0][:, None] == jnp.arange(tenants, dtype=jnp.int32)[None, :]).astype(
        jnp.float32
    )
    row_iota = jnp.arange(row_count, dtype=jnp.int32)
    earlier = (row_iota[None, :] < row_iota[:, None]).astype(jnp.float32)
    before = jnp.dot(earlier, onehot, preferred_element_type=jnp.float32)
    rank_row = jnp.sum(before * onehot, axis=1).astype(jnp.int32)
    slot_row = jnp.sum(onehot * owner[None, :].astype(jnp.float32), axis=1).astype(jnp.int32)
    down_mine = a_half[0]
    up_mine = b_half[0]
    half_cap = capacity // 2
    slots = group_size * half_cap
    target = 2 * slot_row + rank_row % 2
    place = rank_row // 2
    route = placement(target * half_cap + place, slots)
    sent_x = (
        jnp.dot(route, acts, preferred_element_type=jnp.float32)
        .astype(jnp.bfloat16)
        .reshape(group_size, half_cap, width)
    )
    sent_g = (
        jnp.dot(route, grads_out, preferred_element_type=jnp.float32)
        .astype(jnp.bfloat16)
        .reshape(group_size, half_cap, width)
    )
    recv_x, recv_g = (
        lax.all_to_all(sent_x, "dp", split_axis=0, concat_axis=0, tiled=True),
        lax.all_to_all(sent_g, "dp", split_axis=0, concat_axis=0, tiled=True),
    )
    other_down, other_up = from_partner((down_mine, up_mine), "dp", 0)
    down_full = jnp.where(
        first_half,
        jnp.concatenate([down_mine, other_down], axis=0),
        jnp.concatenate([other_down, down_mine], axis=0),
    )
    up_full = jnp.where(
        first_half,
        jnp.concatenate([up_mine, other_up], axis=1),
        jnp.concatenate([other_up, up_mine], axis=1),
    )
    flat_x = recv_x.reshape(-1, width).astype(jnp.float32)
    flat_g = recv_g.reshape(-1, width).astype(jnp.float32)
    hidden_low = exact(flat_x, down_full)
    back_low = exact(flat_g, up_full.T)
    input_rows = 2.0 * exact(back_low, down_full.T)
    returned = lax.all_to_all(
        input_rows.reshape(group_size, half_cap, width),
        "dp",
        split_axis=0,
        concat_axis=0,
        tiled=True,
    )
    input_grad = exact(route.T.astype(jnp.float32), returned.reshape(slots, width))
    down_total = 2.0 * exact(flat_x.T, back_low)
    up_total = 2.0 * exact(hidden_low.T, flat_g)
    keep_down = jnp.where(first_half, down_total[:half_width], down_total[half_width:])
    give_down = jnp.where(first_half, down_total[half_width:], down_total[:half_width])
    keep_up = jnp.where(first_half, up_total[:, :half_width], up_total[:, half_width:])
    give_up = jnp.where(first_half, up_total[:, half_width:], up_total[:, :half_width])
    came_down, came_up = from_partner((give_down, give_up), "dp", 0)
    grad_down = keep_down + came_down
    grad_up = keep_up + came_up
    return (input_grad, grad_down[None], grad_up[None])


def solution(mesh):
    in_specs = (
        P(("groups", "dp"), None),
        P(("groups", "dp"), None),
        P(("groups", "dp"), None),
        P("groups"),
        P(("groups", "dp"), None, None),
        P(("groups", "dp"), None, None),
    )
    out_specs = (
        P(("groups", "dp"), None),
        P(("groups", "dp"), None, None),
        P(("groups", "dp"), None, None),
    )
    return jax.shard_map(body, mesh=mesh, in_specs=in_specs, out_specs=out_specs, check_vma=False)
```

profile of v0, /device:TPU:13, one launch (start us, length us, event | category | flops | bytes accessed | tf_op | source)
XLA Modules:
  0.0 398.9 jit_solution(16836598529630106188)
XLA Ops:
  0.6 1.0 fusion.7
  1.6 0.7 convert_element_type.30
  2.3 0.7 select_reduce_fusion
  3.1 3.3 convolution_convert_fusion.1
  6.3 6.6 %all-to-all-start = ((bf16[16,16,8192]{2,1,0:T(8,128)(2,1)}), bf16[16,16,8192]{2,1,0:T(8,128)(2,1)}, u32[]{:S(2)}, u32[]{:S(2)}) async-start(bf16[16,16,8192]{2,1,0:T(8,128)(2,1)} %bitcast.25), calls=%async_computation | async-start | bytes 8388608 | tf_op jit(solution)/shard_map/all_to_all | solution.py:55
  12.9 4.8 %convolution_convert_fusion = bf16[256,8192]{1,0:T(8,128)(2,1)} fusion(bf16[128,8192]{1,0:T(8,128)(2,1)} %param.6, s32[128]{0:T(128)S(1)} %multiply_add_fusion), kind=kOutput, calls=%fused_computation.1 | convolution fusion | flops 539000832 | bytes 6291968 | tf_op jit(solution)/shard_map/dot_general | solution.py:44
  17.7 87.7 %all-to-all-done = bf16[16,16,8192]{2,1,0:T(8,128)(2,1)} async-done(((bf16[16,16,8192]{2,1,0:T(8,128)(2,1)}), bf16[16,16,8192]{2,1,0:T(8,128)(2,1)}, u32[]{:S(2)}, u32[]{:S(2)}) %all-to-all-start) | async-done | bytes 4194336 | tf_op jit(solution)/shard_map/all_to_all | solution.py:55
  105.3 5.0 %all-to-all-start.2 = ((bf16[16,16,8192]{2,1,0:T(8,128)(2,1)}), bf16[16,16,8192]{2,1,0:T(8,128)(2,1)}, u32[]{:S(2)}, u32[]{:S(2)}) async-start(bf16[16,16,8192]{2,1,0:T(8,128)(2,1)} %bitcast.24), calls=%async_computation.2 | async-start | bytes 8388608 | tf_op jit(solution)/shard_map/all_to_all | solution.py:54
  110.4 0.4 collective-permute-start
  110.9 2.7 collective-permute-done
  113.6 7.4 %fusion = f32[256,64]{0,1:T(8,128)S(1)} fusion(bf16[256,8192]{1,0:T(8,128)(2,1)} %bitcast.2, f32[64,4096]{1,0:T(8,128)} %collective-permute-done, f32[64,4096]{1,0:T(8,128)} %bitcast.30, pred[]{:T(512)S(6)} %eq.42), kind=kOutput, calls=%fused_computation.6 | convolution fusion | flops 1612185600 | bytes 6356993 | tf_op jit(solution)/shard_map/dot_general | solution.py:14
  121.0 10.2 %convolution_multiply_fusion = f32[256,8192]{1,0:T(8,128)} fusion(f32[256,64]{0,1:T(8,128)S(1)} %fusion, f32[4096,64]{0,1:T(8,128)} %collective-permute-done.1, f32[4096,64]{0,1:T(8,128)S(1)} %bitcast.27, pred[]{:T(512)S(6)} %eq.42), kind=kOutput, calls=%fused_computation | convolution fusion | flops 1614282752 | bytes 10551297 | tf_op jit(solution)/shard_map/dot_general | solution.py:14
  131.2 71.7 %all-to-all-done.2 = bf16[16,16,8192]{2,1,0:T(8,128)(2,1)} async-done(((bf16[16,16,8192]{2,1,0:T(8,128)(2,1)}), bf16[16,16,8192]{2,1,0:T(8,128)(2,1)}, u32[]{:S(2)}, u32[]{:S(2)}) %all-to-all-start.2) | async-done | bytes 4194336 | tf_op jit(solution)/shard_map/all_to_all | solution.py:54
  202.8 4.9 %all-to-all-start.1 = ((f32[16,16,8192]{2,1,0:T(8,128)}), f32[16,16,8192]{2,1,0:T(8,128)}, u32[]{:S(2)}, u32[]{:S(2)}) async-start(f32[16,16,8192]{2,1,0:T(8,128)} %bitcast.23), calls=%async_computation.1 | async-start | bytes 16777216 | tf_op jit(solution)/shard_map/all_to_all | solution.py:73
  207.7 6.7 %fusion.6 = f32[256,64]{1,0:T(8,128)S(1)} fusion(bf16[256,8192]{1,0:T(8,128)(2,1)} %bitcast.8, f32[4096,64]{0,1:T(8,128)} %collective-permute-done.1, f32[4096,64]{0,1:T(8,128)S(1)} %bitcast.28, pred[]{:T(512)S(6)} %eq.42), kind=kOutput, calls=%fused_computation.13 | convolution fusion | flops 1612185600 | bytes 6356993 | tf_op jit(solution)/shard_map/dot_general | solution.py:14
  214.4 4.6 %convolution_multiply_fusion.1 = f32[64,8192]{1,0:T(8,128)S(1)} fusion(f32[256,64]{1,0:T(8,128)S(1)} %fusion.6, bf16[256,8192]{1,0:T(8,128)(2,1)} %bitcast.2), kind=kOutput, calls=%fused_computation.3 | convolution fusion | flops 1611137024 | bytes 6356992 | tf_op jit(solution)/shard_map/dot_general | solution.py:14
  219.2 0.4 collective-permute-start.3
  219.6 4.5 %convolution_multiply_fusion.2 = f32[8192,64]{0,1:T(8,128)S(1)} fusion(bf16[256,8192]{1,0:T(8,128)(2,1)} %bitcast.8, f32[256,64]{0,1:T(8,128)S(1)} %fusion), kind=kOutput, calls=%fused_computation.4 | convolution fusion | flops 1611137024 | bytes 6356992 | tf_op jit(solution)/shard_map/dot_general | solution.py:14
  224.2 0.2 collective-permute-start.2
  224.5 1.1 add_bitcast_fusion
  225.6 1.4 collective-permute-done.2
  227.0 1.1 add_bitcast_fusion.1
  228.1 162.0 %all-to-all-done.1 = f32[16,16,8192]{2,1,0:T(8,128)} async-done(((f32[16,16,8192]{2,1,0:T(8,128)}), f32[16,16,8192]{2,1,0:T(8,128)}, u32[]{:S(2)}, u32[]{:S(2)}) %all-to-all-start.1) | async-done | bytes 8388640 | tf_op jit(solution)/shard_map/all_to_all | solution.py:73
  390.1 8.8 %fusion.11 = f32[128,8192]{1,0:T(8,128)} fusion(f32[256,8192]{1,0:T(8,128)} %bitcast.6, s32[128]{0:T(128)S(1)} %multiply_add_fusion), kind=kOutput, calls=%fused_computation.24 | convolution fusion | flops 3221258240 | bytes 12583424 | tf_op jit(solution)/shard_map/dot_general | solution.py:14
  (10 shorter events, 0.4 us)
Async XLA Ops:
  0.6 2.4 copy-start
  6.3 99.0 %all-to-all-start = ((bf16[16,16,8192]{2,1,0:T(8,128)(2,1)}), bf16[16,16,8192]{2,1,0:T(8,128)(2,1)}, u32[]{:S(2)}, u32[]{:S(2)}) async-start(bf16[16,16,8192]{2,1,0:T(8,128)(2,1)} %bitcast.25), calls=%async_computation | async-start | bytes 8388608 | tf_op jit(solution)/shard_map/all_to_all | solution.py:55
  105.3 5.4 %copy-start.1 = (f32[1,4096,64]{1,2,0:T(8,128)S(1)}, f32[1,4096,64]{1,2,0:T(8,128)}, u32[]{:S(2)}) copy-start(f32[1,4096,64]{1,2,0:T(8,128)} %param.10) | copy-start | bytes 3145732
  105.3 97.5 %all-to-all-start.2 = ((bf16[16,16,8192]{2,1,0:T(8,128)(2,1)}), bf16[16,16,8192]{2,1,0:T(8,128)(2,1)}, u32[]{:S(2)}, u32[]{:S(2)}) async-start(bf16[16,16,8192]{2,1,0:T(8,128)(2,1)} %bitcast.24), calls=%async_computation.2 | async-start | bytes 8388608 | tf_op jit(solution)/shard_map/all_to_all | solution.py:54
  110.4 3.2 collective-permute-start
  110.7 10.2 %collective-permute-start.1 = (f32[4096,64]{0,1:T(8,128)S(1)}, f32[4096,64]{0,1:T(8,128)}, u32[]{:S(2)}, u32[]{:S(2)}) collective-permute-start(f32[4096,64]{0,1:T(8,128)S(1)} %bitcast.26), channel_id=1, source_target_pairs={{0,1},{1,0},{2,3},{3,2},{4,5},{5,4},{6,7},{7,6},{8,9},{9,8},{10,11... | collective-permute-start | bytes 3145736 | tf_op jit(solution)/shard_map/ppermute | solution.py:10
  202.8 187.3 %all-to-all-start.1 = ((f32[16,16,8192]{2,1,0:T(8,128)}), f32[16,16,8192]{2,1,0:T(8,128)}, u32[]{:S(2)}, u32[]{:S(2)}) async-start(f32[16,16,8192]{2,1,0:T(8,128)} %bitcast.23), calls=%async_computation.1 | async-start | bytes 16777216 | tf_op jit(solution)/shard_map/all_to_all | solution.py:73
  219.2 5.3 %collective-permute-start.3 = (f32[64,4096]{1,0:T(8,128)S(1)}, f32[64,4096]{1,0:T(8,128)S(1)}, u32[]{:S(2)}, u32[]{:S(2)}) collective-permute-start(f32[64,4096]{1,0:T(8,128)S(1)} %slice_select_fusion), channel_id=1, source_target_pairs={{0,1},{1,0},{2,3},{3,2},{4,5},{5,4},{6,7},{7,6},{8,9},{9,8},{10,11... | collective-permute-start | bytes 3145736 | tf_op jit(solution)/shard_map/ppermute | solution.py:10
  224.2 2.7 collective-permute-start.2
where the time goes:
time: 399 us
  waiting for transfers between devices  325 us (81%)
  matrix products  51.1 us (13%)
  starting transfers between devices  17.7 us (4%)
    all_to_all x1, waiting for transfers between devices, body(): lax.all_to_all(input_rows.reshape(group_size, half_cap, width), 'dp', spl...  162 us
    all_to_all x1, waiting for transfers between devices, body(): lax.all_to_all(sent_g, 'dp', split_axis=0, concat_axis=0, tiled=True)  87.7 us
    all_to_all x1, waiting for transfers between devices, body(): lax.all_to_all(sent_x, 'dp', split_axis=0, concat_axis=0, tiled=True)  71.7 us
    dot_general x6, matrix products, exact(): jnp.dot(left, right, precision=lax.Precision.HIGHEST, preferred_element_t...  42.1 us
  transfers between devices with their start and end apart: 7, of which 5 were waited for; matrix products, arithmetic and copies ran while one was open for 10% of the time, Pallas kernels for 0%

commit v1 on v0

--- a/solution.py
+++ b/solution.py
@@ -90,7 +90,100 @@
     return (input_grad, grad_down[None], grad_up[None])
 
 
+def split_bf16(value):
+    high = lax.reduce_precision(value, exponent_bits=8, mantissa_bits=7)
+    return high.astype(jnp.bfloat16), (value - high).astype(jnp.bfloat16)
+
+
+def mm(left, right, dims):
+    return lax.dot_general(left, right, (dims, ((), ())), preferred_element_type=jnp.float32)
+
+
+def swap(value):
+    return lax.all_to_all(value, "dp", split_axis=0, concat_axis=0, tiled=True)
+
+
+BLOCK = 128
+EXTRA = 16
+
+
+def encode(value):
+    chunks, rows, width = value.shape
+    blocks = width // BLOCK
+    cells = value.reshape(chunks, rows, blocks, BLOCK)
+    peak = jnp.maximum(jnp.max(jnp.abs(cells), axis=3), 1e-30)
+    power = jnp.ceil(jnp.log2(peak * (1.0 / 32000.0)))
+    coded = jnp.round(cells * jnp.exp2(-power)[..., None]).astype(jnp.int16)
+    coded = coded.reshape(chunks, rows, width)
+    powers = power.astype(jnp.int16).reshape(chunks, -1)
+    powers = jnp.pad(powers, ((0, 0), (0, EXTRA * width - powers.shape[1])))
+    return jnp.concatenate([coded, powers.reshape(chunks, EXTRA, width)], axis=1)
+
+
+def decode(coded, rows):
+    chunks, _, width = coded.shape
+    blocks = width // BLOCK
+    powers = coded[:, rows:].reshape(chunks, EXTRA * width)[:, : rows * blocks]
+    scale = jnp.exp2(powers.astype(jnp.float32)).reshape(chunks, rows, blocks, 1)
+    cells = coded[:, :rows].astype(jnp.float32).reshape(chunks, rows, blocks, BLOCK)
+    return (cells * scale).reshape(chunks, rows, width)
+
+
+def by_columns(acts, grads_out, tenant_ids, owner, a_half, b_half):
+    rows, width = acts.shape
+    size = lax.axis_size("dp")
+    slots = owner.shape[0]
+    rank = a_half.shape[2]
+    piece = width // (2 * size)
+    chunk = 2 * piece
+    total = rows * size
+    hit = tenant_ids == jnp.arange(slots, dtype=jnp.int32)[None, :]
+    slot_row = jnp.sum(jnp.where(hit, owner[None, :], 0), axis=1)
+    slot_all = lax.all_gather(slot_row, "dp", tiled=True)
+    mask = slot_all[None, :] == jnp.arange(slots, dtype=jnp.int32)[:, None]
+
+    def adapters(value):
+        sent = value.reshape(rank, size, piece).transpose(1, 0, 2)
+        came = swap(sent).reshape(slots, 2, rank, piece).transpose(0, 2, 1, 3)
+        return split_bf16(came.reshape(slots * rank, chunk))
+
+    def tokens(value):
+        sent = value.reshape(rows, 2, size, piece).transpose(2, 0, 1, 3)
+        return swap(sent.reshape(size, rows, chunk)).reshape(total, chunk)
+
+    def reduced(high, low, value):
+        wide = mm(high, value, ((1,), (1,))) + mm(low, value, ((1,), (1,)))
+        wide = wide.reshape(slots, rank, total)
+        part = jnp.sum(jnp.where(mask[:, None, :], wide, 0.0), axis=0)
+        part = part.reshape(rank, size, rows).transpose(1, 0, 2)
+        mine = jnp.sum(swap(part), axis=0)
+        whole = lax.all_gather(mine, "dp", axis=0).transpose(1, 0, 2).reshape(rank, total)
+        expanded = jnp.where(mask[:, None, :], whole[None], 0.0).reshape(slots * rank, total)
+        return split_bf16(expanded)
+
+    up_high, up_low = adapters(b_half[0])
+    grads = tokens(grads_out)
+    back_high, back_low = reduced(up_high, up_low, grads)
+    down_high, down_low = adapters(a_half[0].T)
+    x = tokens(acts)
+    low_high, low_low = reduced(down_high, down_low, x)
+    dx = mm(back_high, down_high, ((0,), (0,)))
+    dx = dx + (mm(back_low, down_high, ((0,), (0,))) + mm(back_high, down_low, ((0,), (0,))))
+    coded = swap(encode((2.0 * dx).reshape(size, rows, chunk)))
+    input_grad = decode(coded, rows).reshape(size, rows, 2, piece).transpose(1, 2, 0, 3)
+
+    def returned(high, low, value):
+        grad = 2.0 * (mm(high, value, ((1,), (0,))) + mm(low, value, ((1,), (0,))))
+        sent = grad.reshape(slots, rank, 2, piece).transpose(0, 2, 1, 3)
+        return swap(sent.reshape(size, rank, piece)).transpose(1, 0, 2).reshape(rank, size * piece)
+
+    grad_down = returned(back_high, back_low, x)
+    grad_up = returned(low_high, low_low, grads)
+    return (input_grad.reshape(rows, width), grad_down.T[None], grad_up[None])
+
+
 def solution(mesh):
+    dp = mesh.shape["dp"]
     in_specs = (
         P(("groups", "dp"), None),
         P(("groups", "dp"), None),
@@ -104,4 +197,9 @@
         P(("groups", "dp"), None, None),
         P(("groups", "dp"), None, None),
     )
-    return jax.shard_map(body, mesh=mesh, in_specs=in_specs, out_specs=out_specs, check_vma=False)
+
+    def choose(acts, *rest):
+        narrow = acts.shape[1] // (2 * dp) >= BLOCK
+        return (by_columns if narrow else body)(acts, *rest)
+
+    return jax.shard_map(choose, mesh=mesh, in_specs=in_specs, out_specs=out_specs, check_vma=False)

time: 399 us -> 440 us (1.10)
  waiting for transfers between devices: 325 us -> 155 us
  blocking collectives: 0 us -> 99.9 us
  local copies, waits for them, and re-layouts: 0.01 us -> 83 us
  starting transfers between devices: 17.7 us -> 51.1 us
  matrix products: 51.1 us -> 27.3 us
  other arithmetic: 3.9 us -> 20.8 us
    all_to_all x3 -> x9, waiting for transfers between devices: 321 us -> 155 us  [swap(): return lax.all_to_all(value, 'dp', split_axis=0, concat_axis=0, tiled=True)]
    all_gather x0 -> x3, blocking collectives: none -> 99.9 us  [the longest x1 56.7 us: by_columns(): slot_all = lax.all_gather(slot_row, 'dp', tiled=True)]
    all_to_all x3 -> x9, starting transfers between devices: 16.5 us -> 51.1 us  [swap(): return lax.all_to_all(value, 'dp', split_axis=0, concat_axis=0, tiled=True)]
    dot_general x9 -> x11, matrix products: 51.1 us -> 27.3 us  [mm(): lax.dot_general(left, right, (dims, ((), ())), preferred_element_type=jnp...]
    unnamed x4 -> x39, local copies, waits for them, and re-layouts: 0.01 us -> 21.9 us
    reshape x0 -> x7, local copies, waits for them, and re-layouts: none -> 19.6 us  [the longest x4 10.5 us: returned(): sent = grad.reshape(slots, rank, 2, piece).transpose(0, 2, 1, 3)]
    transpose x0 -> x8, local copies, waits for them, and re-layouts: none -> 13.8 us  [the longest x2 4.61 us: tokens(): sent = value.reshape(rows, 2, size, piece).transpose(2, 0, 1, 3)]
    mul x0 -> x4, local copies, waits for them, and re-layouts: none -> 9.69 us  [the longest x2 9.3 us: encode(): coded = jnp.round(cells * jnp.exp2(-power)[..., None]).astype(jnp.int16)]
  transfers between devices with their start and end apart: 7 -> 9, of which waited for: 5 -> 6; matrix products, arithmetic and copies ran while one was open for 10% -> 19% of each run, Pallas kernels for 0% -> 0%
where the time goes in v1:
time: 440 us; the launch traced here: 438 us
  waiting for transfers between devices  155 us (35%)
  blocking collectives  99.9 us (23%)
  local copies, waits for them, and re-layouts  83 us (19%)
  starting transfers between devices  51.1 us (12%)
  matrix products  27.3 us (6%)
  other arithmetic  20.8 us (5%)
    all_to_all x9, waiting for transfers between devices, swap(): return lax.all_to_all(value, 'dp', split_axis=0, concat_axis=0, tiled=True)  155 us
    all_gather x1, blocking collectives, by_columns(): slot_all = lax.all_gather(slot_row, 'dp', tiled=True)  56.7 us
    all_to_all x9, starting transfers between devices, swap(): return lax.all_to_all(value, 'dp', split_axis=0, concat_axis=0, tiled=True)  51.1 us
    all_gather x2, blocking collectives, reduced(): lax.all_gather(mine, 'dp', axis=0).transpose(1, 0, 2).reshape(rank, total)  43.2 us
    dot_general x11, matrix products, mm(): lax.dot_general(left, right, (dims, ((), ())), preferred_element_type=jnp...  27.3 us
    unnamed x39, local copies, waits for them, and re-layouts  21.9 us
    reshape x4, local copies, waits for them, and re-layouts, returned(): sent = grad.reshape(slots, rank, 2, piece).transpose(0, 2, 1, 3)  10.5 us
    mul x2, local copies, waits for them, and re-layouts, encode(): coded = jnp.round(cells * jnp.exp2(-power)[..., None]).astype(jnp.int16)  9.3 us
  transfers between devices with their start and end apart: 9, of which 6 were waited for; matrix products, arithmetic and copies ran while one was open for 19% of the time, Pallas kernels for 0%

profile of v1, /device:TPU:13, one launch (start us, length us, event | category | flops | bytes accessed | tf_op | source)
XLA Modules:
  0.0 438.0 jit_solution(15435215722776658422)
XLA Ops:
  3.8 6.6 %all-to-all-start.3 = ((f32[16,64,256]{2,1,0:T(8,128)}), f32[16,64,256]{2,1,0:T(8,128)S(1)}, u32[]{:S(2)}, u32[]{:S(2)}) async-start(f32[16,64,256]{2,1,0:T(8,128)} %copy.152), calls=%async_computation.3 | async-start | bytes 2097152 | tf_op jit(solution)/shard_map/all_to_all | solution.py:103
  12.2 23.0 %all-to-all-done.3 = f32[16,64,256]{2,1,0:T(8,128)S(1)} async-done(((f32[16,64,256]{2,1,0:T(8,128)}), f32[16,64,256]{2,1,0:T(8,128)S(1)}, u32[]{:S(2)}, u32[]{:S(2)}) %all-to-all-start.3) | async-done | bytes 1048608 | tf_op jit(solution)/shard_map/all_to_all | solution.py:103
  35.2 4.9 %all-to-all-start = ((f32[16,64,256]{2,1,0:T(8,128)}), f32[16,64,256]{2,1,0:T(8,128)}, u32[]{:S(2)}, u32[]{:S(2)}) async-start(f32[16,64,256]{2,1,0:T(8,128)} %copy.144), calls=%async_computation | async-start | bytes 2097152 | tf_op jit(solution)/shard_map/all_to_all | solution.py:103
  44.8 20.3 %all-to-all-done = f32[16,64,256]{2,1,0:T(8,128)} async-done(((f32[16,64,256]{2,1,0:T(8,128)}), f32[16,64,256]{2,1,0:T(8,128)}, u32[]{:S(2)}, u32[]{:S(2)}) %all-to-all-start) | async-done | bytes 1048608 | tf_op jit(solution)/shard_map/all_to_all | solution.py:103
  65.1 4.9 %all-to-all-start.1 = ((bf16[16,128,512]{1,2,0:T(8,128)(2,1)}), bf16[16,128,512]{1,2,0:T(8,128)(2,1)S(1)}, u32[]{:S(2)}, u32[]{:S(2)}) async-start(bf16[16,128,512]{1,2,0:T(8,128)(2,1)} %bitcast.145), calls=%async_computation.1 | async-start | bytes 4194304 | tf_op jit(solution)/shard_map/all_to_all | solution.py:103
  77.3 40.2 %all-to-all-done.1 = bf16[16,128,512]{1,2,0:T(8,128)(2,1)S(1)} async-done(((bf16[16,128,512]{1,2,0:T(8,128)(2,1)}), bf16[16,128,512]{1,2,0:T(8,128)(2,1)S(1)}, u32[]{:S(2)}, u32[]{:S(2)}) %all-to-all-start.1) | async-done | bytes 2097184 | tf_op jit(solution)/shard_map/all_to_all | solution.py:103
  118.8 4.9 %all-to-all-start.5 = ((bf16[16,128,512]{1,2,0:T(8,128)(2,1)}), bf16[16,128,512]{1,2,0:T(8,128)(2,1)}, u32[]{:S(2)}, u32[]{:S(2)}) async-start(bf16[16,128,512]{1,2,0:T(8,128)(2,1)} %bitcast.144), calls=%async_computation.5 | async-start | bytes 4194304 | tf_op jit(solution)/shard_map/all_to_all | solution.py:103
  123.8 56.7 %all-gather.2 = s32[16,1,128]{2,1,0:T(1,128)S(1)} all-gather(s32[1,1,128]{2,1,0:T(1,128)S(1)} %bitcast.178), channel_id=1, replica_groups=mesh['groups'=2,'dp'=16] {'dp'}, dimensions={0}, use_global_device_ids=true | all-gather | bytes 8704 | tf_op jit(solution)/shard_map/all_gather | solution.py:142
  203.8 5.0 %all-to-all-start.7 = ((f32[16,64,128]{2,1,0:T(8,128)}), f32[16,64,128]{2,1,0:T(8,128)S(1)}, u32[]{:S(2)}, u32[]{:S(2)}) async-start(f32[16,64,128]{2,1,0:T(8,128)} %copy.168), calls=%async_computation.7 | async-start | bytes 1048576 | tf_op jit(solution)/shard_map/all_to_all | solution.py:103
  209.9 12.5 %all-to-all-done.7 = f32[16,64,128]{2,1,0:T(8,128)S(1)} async-done(((f32[16,64,128]{2,1,0:T(8,128)}), f32[16,64,128]{2,1,0:T(8,128)S(1)}, u32[]{:S(2)}, u32[]{:S(2)}) %all-to-all-start.7) | async-done | bytes 524320 | tf_op jit(solution)/shard_map/all_to_all | solution.py:103
  222.4 5.0 %all-to-all-start.2 = ((f32[16,64,128]{2,1,0:T(8,128)}), f32[16,64,128]{2,1,0:T(8,128)S(1)}, u32[]{:S(2)}, u32[]{:S(2)}) async-start(f32[16,64,128]{2,1,0:T(8,128)} %copy.150), calls=%async_computation.2 | async-start | bytes 1048576 | tf_op jit(solution)/shard_map/all_to_all | solution.py:103
  227.4 25.2 %all-gather.1 = f32[1024,128]{1,0:T(8,128)S(1)} all-gather(f32[64,128]{1,0:T(8,128)S(1)} %reduce_sum.49), channel_id=3, replica_groups=mesh['groups'=2,'dp'=16] {'dp'}, dimensions={0}, use_global_device_ids=true | all-gather | bytes 557056 | tf_op jit(solution)/shard_map/all_gather | solution.py:160
  253.5 18.0 %all-gather = f32[1024,128]{1,0:T(8,128)S(1)} all-gather(f32[64,128]{1,0:T(8,128)S(1)} %reduce_sum.47), channel_id=2, replica_groups=mesh['groups'=2,'dp'=16] {'dp'}, dimensions={0}, use_global_device_ids=true | all-gather | bytes 557056 | tf_op jit(solution)/shard_map/all_gather | solution.py:160
  284.0 8.9 %all-to-all-start.8 = ((f32[16,64,256]{2,1,0:T(8,128)}), f32[16,64,256]{2,1,0:T(8,128)}, u32[]{:S(2)}, u32[]{:S(2)}) async-start(f32[16,64,256]{2,1,0:T(8,128)} %bitcast.152), calls=%async_computation.8 | async-start | bytes 2097152 | tf_op jit(solution)/shard_map/all_to_all | solution.py:103
  306.8 11.1 %all-to-all-done.8 = f32[16,64,256]{2,1,0:T(8,128)} async-done(((f32[16,64,256]{2,1,0:T(8,128)}), f32[16,64,256]{2,1,0:T(8,128)}, u32[]{:S(2)}, u32[]{:S(2)}) %all-to-all-start.8) | async-done | bytes 1048608 | tf_op jit(solution)/shard_map/all_to_all | solution.py:103
  318.0 4.9 %all-to-all-start.6 = ((f32[16,64,256]{2,1,0:T(8,128)}), f32[16,64,256]{2,1,0:T(8,128)}, u32[]{:S(2)}, u32[]{:S(2)}) async-start(f32[16,64,256]{2,1,0:T(8,128)} %bitcast.150), calls=%async_computation.6 | async-start | bytes 2097152 | tf_op jit(solution)/shard_map/all_to_all | solution.py:103
  325.1 5.2 %fusion.8 = (f32[2048,512]{1,0:T(8,128)}, f32[2048,512]{1,0:T(8,128)}) fusion(f32[2048,512]{1,0:T(8,128)S(1)} %fusion.10, f32[2048,512]{1,0:T(8,128)S(1)} %copy-done, bf16[512,2048]{1,0:T(8,128)(2,1)S(1)} %bitcast.123, bf16[512,512]{1,0:T(8,128)(2,1)S(1)} %bitcast.149), kind=kOutput, calls=%fused_computation.35 | convolution fusion | flops 1077936128 | bytes 19398656 | tf_op jit(solution)/shard_map/dot_general | solution.py:99
  330.3 5.3 %abs.7 = f32[16,128,4,128]{3,2,1,0:T(4,128)} reshape(f32[2048,512]{1,0:T(8,128)} %get-tuple-element.35) | data formatting | bytes 8388608 | tf_op jit(solution)/shard_map/abs | solution.py:114
  346.5 5.5 %mul.53 = f32[16,128,512]{2,1,0:T(8,128)} reshape(f32[16,128,4,128]{3,2,1,0:T(4,128)} %mul.52) | data formatting | bytes 8388608 | tf_op jit(solution)/shard_map/mul | solution.py:116
  352.0 4.6 %round-nearest-even_convert_fusion = s16[16,128,512]{2,1,0:T(8,128)(2,1)S(1)} fusion(f32[16,128,512]{2,1,0:T(8,128)} %bitcast.132, f32[16,128,512]{2,1,0:T(8,128)} %mul.53), kind=kLoop, calls=%fused_computation.9 | loop fusion | flops 3145728 | bytes 10485760 | tf_op jit(solution)/shard_map/convert_element_type | solution.py:116
  358.3 6.0 %all-to-all-start.4 = ((s16[16,144,512]{2,1,0:T(8,128)(2,1)}), s16[16,144,512]{2,1,0:T(8,128)(2,1)S(1)}, u32[]{:S(2)}, u32[]{:S(2)}) async-start(s16[16,144,512]{2,1,0:T(8,128)(2,1)} %pad_add_fusion), calls=%async_computation.4 | async-start | bytes 4718592 | tf_op jit(solution)/shard_map/all_to_all | solution.py:103
  369.6 47.7 %all-to-all-done.4 = s16[16,144,512]{2,1,0:T(8,128)(2,1)S(1)} async-done(((s16[16,144,512]{2,1,0:T(8,128)(2,1)}), s16[16,144,512]{2,1,0:T(8,128)(2,1)S(1)}, u32[]{:S(2)}, u32[]{:S(2)}) %all-to-all-start.4) | async-done | bytes 2359328 | tf_op jit(solution)/shard_map/all_to_all | solution.py:103
  420.0 5.3 %copy.159 = f32[16,128,512]{1,2,0:T(8,128)} copy(f32[16,128,512]{2,1,0:T(8,128)} %slice_convert_fusion) | data formatting | bytes 8388608 | tf_op jit(solution)/shard_map/reshape | solution.py:128
  432.4 5.6 %copy.172 = f32[128,8192]{1,0:T(8,128)} copy(f32[128,8192]{0,1:T(8,128)} %bitcast.137) | data formatting | bytes 8388608
  (97 shorter events, 99.6 us)
Async XLA Ops:
  2.2 8.2 %copy-start.11 = (f32[1,64,4096]{2,1,0:T(8,128)S(1)}, f32[1,64,4096]{2,1,0:T(8,128)}, u32[]{:S(2)}) copy-start(f32[1,64,4096]{2,1,0:T(8,128)} %param.11) | copy-start | bytes 3145732
  3.8 31.4 %all-to-all-start.3 = ((f32[16,64,256]{2,1,0:T(8,128)}), f32[16,64,256]{2,1,0:T(8,128)S(1)}, u32[]{:S(2)}, u32[]{:S(2)}) async-start(f32[16,64,256]{2,1,0:T(8,128)} %copy.152), calls=%async_computation.3 | async-start | bytes 2097152 | tf_op jit(solution)/shard_map/all_to_all | solution.py:103
  35.2 29.9 %all-to-all-start = ((f32[16,64,256]{2,1,0:T(8,128)}), f32[16,64,256]{2,1,0:T(8,128)}, u32[]{:S(2)}, u32[]{:S(2)}) async-start(f32[16,64,256]{2,1,0:T(8,128)} %copy.144), calls=%async_computation | async-start | bytes 2097152 | tf_op jit(solution)/shard_map/all_to_all | solution.py:103
  65.1 52.4 %all-to-all-start.1 = ((bf16[16,128,512]{1,2,0:T(8,128)(2,1)}), bf16[16,128,512]{1,2,0:T(8,128)(2,1)S(1)}, u32[]{:S(2)}, u32[]{:S(2)}) async-start(bf16[16,128,512]{1,2,0:T(8,128)(2,1)} %bitcast.145), calls=%async_computation.1 | async-start | bytes 4194304 | tf_op jit(solution)/shard_map/all_to_all | solution.py:103
  117.5 1.3 copy-start.9
  117.5 6.2 %copy-start.12 = (s32[8]{0:T(128)S(1)}, s32[8]{0:T(128)}, u32[]{:S(2)}) copy-start(s32[8]{0:T(128)} %param.9) | copy-start | bytes 100
  117.5 6.2 %copy-start.13 = (s32[128,1]{0,1:T(1,128)S(1)}, s32[128,1]{0,1:T(1,128)}, u32[]{:S(2)}) copy-start(s32[128,1]{0,1:T(1,128)} %param.8) | copy-start | bytes 1540
  118.8 76.5 %all-to-all-start.5 = ((bf16[16,128,512]{1,2,0:T(8,128)(2,1)}), bf16[16,128,512]{1,2,0:T(8,128)(2,1)}, u32[]{:S(2)}, u32[]{:S(2)}) async-start(bf16[16,128,512]{1,2,0:T(8,128)(2,1)} %bitcast.144), calls=%async_computation.5 | async-start | bytes 4194304 | tf_op jit(solution)/shard_map/all_to_all | solution.py:103
  189.1 2.8 copy-start.3
  189.1 2.8 copy-start.10
  198.2 1.3 copy-start.1
  199.5 2.2 copy-start.6
  203.8 18.6 %all-to-all-start.7 = ((f32[16,64,128]{2,1,0:T(8,128)}), f32[16,64,128]{2,1,0:T(8,128)S(1)}, u32[]{:S(2)}, u32[]{:S(2)}) async-start(f32[16,64,128]{2,1,0:T(8,128)} %copy.168), calls=%async_computation.7 | async-start | bytes 1048576 | tf_op jit(solution)/shard_map/all_to_all | solution.py:103
  222.4 31.1 %all-to-all-start.2 = ((f32[16,64,128]{2,1,0:T(8,128)}), f32[16,64,128]{2,1,0:T(8,128)S(1)}, u32[]{:S(2)}, u32[]{:S(2)}) async-start(f32[16,64,128]{2,1,0:T(8,128)} %copy.150), calls=%async_computation.2 | async-start | bytes 1048576 | tf_op jit(solution)/shard_map/all_to_all | solution.py:103
  271.6 3.8 copy-start.4
  284.0 33.9 %all-to-all-start.8 = ((f32[16,64,256]{2,1,0:T(8,128)}), f32[16,64,256]{2,1,0:T(8,128)}, u32[]{:S(2)}, u32[]{:S(2)}) async-start(f32[16,64,256]{2,1,0:T(8,128)} %bitcast.152), calls=%async_computation.8 | async-start | bytes 2097152 | tf_op jit(solution)/shard_map/all_to_all | solution.py:103
  293.0 3.0 copy-start.2
  293.0 3.0 copy-start.7
  301.0 2.5 copy-start.8
  318.0 40.3 %all-to-all-start.6 = ((f32[16,64,256]{2,1,0:T(8,128)}), f32[16,64,256]{2,1,0:T(8,128)}, u32[]{:S(2)}, u32[]{:S(2)}) async-start(f32[16,64,256]{2,1,0:T(8,128)} %bitcast.150), calls=%async_computation.6 | async-start | bytes 2097152 | tf_op jit(solution)/shard_map/all_to_all | solution.py:103
  322.9 2.2 copy-start
  358.3 59.1 %all-to-all-start.4 = ((s16[16,144,512]{2,1,0:T(8,128)(2,1)}), s16[16,144,512]{2,1,0:T(8,128)(2,1)S(1)}, u32[]{:S(2)}, u32[]{:S(2)}) async-start(s16[16,144,512]{2,1,0:T(8,128)(2,1)} %pad_add_fusion), calls=%async_computation.4 | async-start | bytes 4718592 | tf_op jit(solution)/shard_map/all_to_all | solution.py:103
  427.3 2.2 copy-start.5

commit v2 on v0

--- a/solution.py
+++ b/solution.py
@@ -1,6 +1,10 @@
+import functools
+
 import jax
 import jax.numpy as jnp
 from jax import lax
+from jax.experimental import pallas as pl
+from jax.experimental.pallas import tpu as pltpu
 from jax.sharding import PartitionSpec as P
 
 
@@ -90,7 +94,342 @@
     return (input_grad, grad_down[None], grad_up[None])
 
 
+def mm(left, right, dims):
+    return lax.dot_general(left, right, (dims, ((), ())), preferred_element_type=jnp.float32)
+
+
+MESH = pl.DeviceIdType.MESH
+
+
+def kernel(
+    size,
+    slots,
+    slot_mine,
+    acts,
+    grads_out,
+    down,
+    up,
+    input_grad,
+    grad_down,
+    grad_up,
+    slot_all,
+    tok,
+    adapt,
+    weight,
+    spread,
+    part,
+    red,
+    full,
+    coded,
+    scale,
+    coded_in,
+    scale_in,
+    acc,
+    slot_send,
+    slot_recv,
+    tok_send,
+    tok_recv,
+    adapt_send,
+    adapt_recv,
+    part_send,
+    part_recv,
+    full_send,
+    full_recv,
+    dx_send,
+    dx_recv,
+    grad_send,
+    grad_recv,
+    local,
+):
+    me = lax.axis_index("dp")
+    rows, width = acts.shape
+    rank = down.shape[0]
+    half = width // 2
+    piece = half // size
+    wide_rank = slots * rank
+    tokens = (acts, grads_out)
+    halves = (down, up)
+    grads = (grad_down, grad_up)
+
+    def peer(step):
+        return lax.rem(me + step, size)
+
+    def source(step):
+        return lax.rem(me + size - step, size)
+
+    def each(body_of):
+        lax.fori_loop(1, size, lambda step, carry: (body_of(step), carry)[1], 0)
+
+    def lanes(index, count):
+        return pl.ds(pl.multiple_of(index * count, 128), count)
+
+    def band(index, count):
+        return pl.ds(pl.multiple_of(index * count, 64), count)
+
+    def copy_to(src, dst, send, recv, dev):
+        return pltpu.make_async_remote_copy(
+            src_ref=src, dst_ref=dst, send_sem=send, recv_sem=recv,
+            device_id={"dp": dev}, device_id_type=MESH,
+        )
+
+    def slot_copy(dev, at):
+        return copy_to(slot_mine, slot_all.at[at], slot_send.at[dev], slot_recv.at[at], dev)
+
+    def tok_copy(k, h, dev, at):
+        return copy_to(
+            tokens[k].at[:, pl.ds(pl.multiple_of(h * half + dev * piece, 128), piece)],
+            tok.at[k, band(at, rows), pl.ds(h * piece, piece)],
+            tok_send.at[k, dev, h], tok_recv.at[k, at, h], dev,
+        )
+
+    def adapt_place(k, at):
+        return adapt.at[k, band(at // 2, rank), lanes(lax.rem(at, 2), piece)]
+
+    def adapt_copy(k, dev, at):
+        return copy_to(
+            halves[k].at[:, lanes(dev, piece)], adapt_place(k, at),
+            adapt_send.at[k, dev], adapt_recv.at[k, at], dev,
+        )
+
+    def part_copy(k, dev, at):
+        return copy_to(
+            part.at[k, dev], red.at[k, at], part_send.at[k, dev], part_recv.at[k, at], dev
+        )
+
+    def full_copy(k, dev, at, own):
+        return copy_to(
+            full.at[k, own], full.at[k, at], full_send.at[k, dev], full_recv.at[k, at], dev
+        )
+
+    def coded_copy(dev, at):
+        return copy_to(coded.at[dev], coded_in.at[at], dx_send.at[0, dev], dx_recv.at[0, at], dev)
+
+    def scale_copy(dev, at):
+        return copy_to(scale.at[dev], scale_in.at[at], dx_send.at[1, dev], dx_recv.at[1, at], dev)
+
+    def grad_piece(k, dev):
+        return acc.at[k, band(dev // 2, rank), lanes(lax.rem(dev, 2), piece)]
+
+    def grad_copy(k, dev, at):
+        return copy_to(
+            grad_piece(k, dev), grads[k].at[:, lanes(at, piece)],
+            grad_send.at[k, dev], grad_recv.at[k, at], dev,
+        )
+
+    barrier = pltpu.get_barrier_semaphore()
+    each(lambda step: pl.semaphore_signal(
+        barrier, inc=1, device_id={"dp": peer(step)}, device_id_type=MESH))
+    pl.semaphore_wait(barrier, size - 1)
+
+    each(lambda step: slot_copy(peer(step), me).start())
+    own = []
+    for k in (1, 0):
+        each(lambda step: adapt_copy(k, peer(step), me).start())
+
+        def start_tokens(step):
+            for h in range(2):
+                tok_copy(k, h, peer(step), me).start()
+
+        each(start_tokens)
+        own.append(pltpu.make_async_copy(
+            halves[k].at[:, lanes(me, piece)], adapt_place(k, me), local.at[k, 2]))
+        for h in range(2):
+            own.append(pltpu.make_async_copy(
+                tokens[k].at[:, pl.ds(pl.multiple_of(h * half + me * piece, 128), piece)],
+                tok.at[k, band(me, rows), pl.ds(h * piece, piece)], local.at[k, h]))
+    for one in own:
+        one.start()
+    for one in own:
+        one.wait()
+    slot_all[me] = slot_mine[...]
+    each(lambda step: slot_copy(peer(step), source(step)).wait_recv())
+
+    def high_low(value):
+        high = value.astype(jnp.bfloat16).astype(jnp.float32)
+        return high, value - high
+
+    def partial(k, at):
+        wide = mm(weight[k], tok[k, band(at, rows), :], ((1,), (1,)))
+        ids = slot_all[at][0:1, :]
+        total = jnp.zeros((rank, rows), jnp.float32)
+        for s in range(slots):
+            value = wide[s * rank:(s + 1) * rank]
+            value = value + wide[wide_rank + s * rank:wide_rank + (s + 1) * rank]
+            total = total + jnp.where(ids == s, value, 0.0)
+        return total
+
+    def project(k):
+        each(lambda step: adapt_copy(k, peer(step), source(step)).wait_recv())
+        for s in range(slots):
+            high, low = high_low(adapt[k, s * rank:(s + 1) * rank, :])
+            weight[k, s * rank:(s + 1) * rank, :] = high.astype(jnp.bfloat16)
+            weight[k, wide_rank + s * rank:wide_rank + (s + 1) * rank, :] = low.astype(jnp.bfloat16)
+        red[k, me] = partial(k, me)
+
+        def one(step):
+            at = source(step)
+            for h in range(2):
+                tok_copy(k, h, peer(step), at).wait_recv()
+            part[k, at] = partial(k, at)
+            part_copy(k, at, me).start()
+
+        each(one)
+
+    def combine(k):
+        each(lambda step: part_copy(k, peer(step), source(step)).wait_recv())
+        full[k, me] = jnp.sum(red[k], axis=0)
+        each(lambda step: full_copy(k, peer(step), me, me).start())
+
+    def expand(k, at):
+        ids = slot_all[at][0:1, :]
+        high, low = high_low(full[k, at])
+        for s in range(slots):
+            spread[k, s * rank:(s + 1) * rank, lanes(at, rows)] = jnp.where(
+                ids == s, high, 0.0).astype(jnp.bfloat16)
+            spread[k, wide_rank + s * rank:wide_rank + (s + 1) * rank, lanes(at, rows)] = jnp.where(
+                ids == s, low, 0.0).astype(jnp.bfloat16)
+
+    project(1)
+    combine(1)
+    project(0)
+    combine(0)
+
+    def rows_grad(at, into, into_scale, dev):
+        expand(1, at)
+        high = spread[1, :wide_rank, lanes(at, rows)]
+        low = spread[1, wide_rank:, lanes(at, rows)]
+        dx = mm(high, weight[0, :wide_rank, :], ((0,), (0,)))
+        dx = dx + mm(low, weight[0, :wide_rank, :], ((0,), (0,)))
+        dx = 2.0 * (dx + mm(high, weight[0, wide_rank:, :], ((0,), (0,))))
+        peak = jnp.maximum(jnp.max(jnp.abs(dx), axis=0, keepdims=True), 1e-30)
+        value = jnp.floor(dx * (32700.0 / peak) + 0.5)
+        into[dev] = value.astype(jnp.int32).astype(jnp.int16)
+        unit = peak * (1.0 / 32700.0)
+        for q in range(2 * piece // 128):
+            into_scale[dev, q:q + 1, :] = unit[:, q * 128:(q + 1) * 128]
+
+    rows_grad(me, coded_in, scale_in, me)
+
+    def send_rows(step):
+        at = source(step)
+        full_copy(1, peer(step), at, me).wait_recv()
+        rows_grad(at, coded, scale, at)
+        coded_copy(at, me).start()
+        scale_copy(at, me).start()
+
+    each(send_rows)
+
+    def weight_grad(k):
+        def column(h, carry):
+            value = mm(spread[1 - k], tok[k, :, lanes(h, piece)], ((1,), (0,)))
+            acc[k, :, lanes(h, piece)] = 2.0 * (value[:wide_rank] + value[wide_rank:])
+            return carry
+
+        lax.fori_loop(0, 2, column, 0)
+        grads[k][:, lanes(me, piece)] = grad_piece(k, me)[...]
+        each(lambda step: grad_copy(k, peer(step), me).start())
+
+    weight_grad(0)
+    expand(0, me)
+
+    def low_rows(step):
+        at = source(step)
+        full_copy(0, peer(step), at, me).wait_recv()
+        expand(0, at)
+
+    each(low_rows)
+    weight_grad(1)
+
+    def decode(at):
+        for q in range(2 * piece // 128):
+            h, r = divmod(q * 128, piece)
+            value = coded_in[at, :, q * 128:(q + 1) * 128].astype(jnp.int32).astype(jnp.float32)
+            start = pl.multiple_of(h * half + at * piece + r, 128)
+            input_grad[:, pl.ds(start, 128)] = value * scale_in[at, q:q + 1, :]
+
+    decode(me)
+
+    def take(step):
+        at = source(step)
+        coded_copy(peer(step), at).wait_recv()
+        scale_copy(peer(step), at).wait_recv()
+        decode(at)
+
+    each(take)
+
+    def finish(step):
+        dev, at = peer(step), source(step)
+        for k in range(2):
+            grad_copy(k, dev, at).wait_recv()
+            grad_copy(k, dev, me).wait_send()
+            for h in range(2):
+                tok_copy(k, h, dev, me).wait_send()
+            adapt_copy(k, dev, me).wait_send()
+            part_copy(k, dev, me).wait_send()
+            full_copy(k, dev, me, me).wait_send()
+        slot_copy(dev, me).wait_send()
+        coded_copy(dev, me).wait_send()
+        scale_copy(dev, me).wait_send()
+
+    each(finish)
+
+
+def by_columns(acts, grads_out, tenant_ids, owner, a_half, b_half):
+    rows, width = acts.shape
+    size = lax.axis_size("dp")
+    slots = owner.shape[0]
+    rank = a_half.shape[2]
+    chunk = width // size
+    total = rows * size
+    hit = tenant_ids == jnp.arange(slots, dtype=jnp.int32)[None, :]
+    slot_row = jnp.sum(jnp.where(hit, owner[None, :], 0), axis=1)
+    slot_mine = jnp.broadcast_to(slot_row[None, :], (8, rows))
+    vmem = pl.BlockSpec(memory_space=pltpu.VMEM)
+    hbm = pl.BlockSpec(memory_space=pl.ANY)
+    dma = pltpu.SemaphoreType.DMA
+    f32, bf16 = jnp.float32, jnp.bfloat16
+    input_grad, grad_down, grad_up = pl.pallas_call(
+        functools.partial(kernel, size, slots),
+        out_shape=(
+            jax.ShapeDtypeStruct((rows, width), f32),
+            jax.ShapeDtypeStruct((rank, width // 2), f32),
+            jax.ShapeDtypeStruct((rank, width // 2), f32),
+        ),
+        in_specs=[vmem, hbm, hbm, hbm, hbm],
+        out_specs=(vmem, vmem, vmem),
+        scratch_shapes=[
+            pltpu.VMEM((size, 8, rows), jnp.int32),
+            pltpu.VMEM((2, total, chunk), bf16),
+            pltpu.VMEM((2, slots * rank, chunk), f32),
+            pltpu.VMEM((2, 2 * slots * rank, chunk), bf16),
+            pltpu.VMEM((2, 2 * slots * rank, total), bf16),
+            pltpu.VMEM((2, size, rank, rows), f32),
+            pltpu.VMEM((2, size, rank, rows), f32),
+            pltpu.VMEM((2, size, rank, rows), f32),
+            pltpu.VMEM((size, rows, chunk), jnp.int16),
+            pltpu.VMEM((size, 8, 128), f32),
+            pltpu.VMEM((size, rows, chunk), jnp.int16),
+            pltpu.VMEM((size, 8, 128), f32),
+            pltpu.VMEM((2, slots * rank, chunk), f32),
+            dma((size,)), dma((size,)),
+            dma((2, size, 2)), dma((2, size, 2)),
+            dma((2, size)), dma((2, size)),
+            dma((2, size)), dma((2, size)),
+            dma((2, size)), dma((2, size)),
+            dma((2, size)), dma((2, size)),
+            dma((2, size)), dma((2, size)),
+            dma((2, 3)),
+        ],
+        compiler_params=pltpu.CompilerParams(
+            collective_id=0, has_side_effects=True, vmem_limit_bytes=56 * 2**20
+        ),
+        name="adapter_backward",
+    )(slot_mine, acts, grads_out, a_half[0].T, b_half[0])
+    return input_grad, grad_down.T[None], grad_up[None]
+
+
 def solution(mesh):
+    dp = mesh.shape["dp"]
     in_specs = (
         P(("groups", "dp"), None),
         P(("groups", "dp"), None),
@@ -104,4 +443,9 @@
         P(("groups", "dp"), None, None),
         P(("groups", "dp"), None, None),
     )
-    return jax.shard_map(body, mesh=mesh, in_specs=in_specs, out_specs=out_specs, check_vma=False)
+
+    def choose(acts, *rest):
+        narrow = acts.shape[1] // (2 * dp) % 128 == 0
+        return (by_columns if narrow else body)(acts, *rest)
+
+    return jax.shard_map(choose, mesh=mesh, in_specs=in_specs, out_specs=out_specs, check_vma=False)

time: 399 us -> 295 us (0.74)
  waiting for transfers between devices: 325 us -> 0 us
  Pallas kernels: 0 us -> 286 us
  matrix products: 51.1 us -> 0 us
  starting transfers between devices: 17.7 us -> 0 us
  local copies, waits for them, and re-layouts: 0.01 us -> 7.3 us
    all_to_all x3 -> x0, waiting for transfers between devices: 321 us -> none  [the longest x1 162 us: body(): lax.all_to_all(input_rows.reshape(group_size, half_cap, width), 'dp', spl...]
    pallas_call x0 -> x1, Pallas kernels: none -> 286 us  [by_columns(): pl.pallas_call(functools.partial(kernel, size, slots), out_shape=(jax.Sha...]
    dot_general x9 -> x0, matrix products: 51.1 us -> none  [the longest x6 42.1 us: exact(): jnp.dot(left, right, precision=lax.Precision.HIGHEST, preferred_element_t...]
    all_to_all x3 -> x0, starting transfers between devices: 16.5 us -> none  [the longest x1 6.55 us: body(): lax.all_to_all(sent_g, 'dp', split_axis=0, concat_axis=0, tiled=True)]
    unnamed x4 -> x7, local copies, waits for them, and re-layouts: 0.01 us -> 6.7 us
    ppermute x4 -> x0, waiting for transfers between devices: 4.1 us -> none  [from_partner(): return lax.ppermute(value, axis, pairs)]
  transfers between devices with their start and end apart: 7 -> 0, of which waited for: 5 -> 0; matrix products, arithmetic and copies ran while one was open for 10% -> 0% of each run, Pallas kernels for 0% -> 0%
where the time goes in v2:
time: 295 us
  Pallas kernels  286 us (97%)
  local copies, waits for them, and re-layouts  7.3 us (2%)
    pallas_call x1, Pallas kernels, by_columns(): pl.pallas_call(functools.partial(kernel, size, slots), out_shape=(jax.Sha...  286 us
    unnamed x7, local copies, waits for them, and re-layouts  6.7 us

profile of v2, /device:TPU:13, one launch (start us, length us, event | category | flops | bytes accessed | tf_op | source)
XLA Modules:
  0.0 294.9 jit_solution(12369522027450933229)
XLA Ops:
  0.6 0.8 select_reduce_fusion
  1.4 0.6 broadcast_in_dim.28.slot_mine
  2.0 286.2 %adapter_backward.1 = (f32[128,8192]{1,0:T(8,128)}, f32[64,4096]{1,0:T(8,128)}, f32[64,4096]{1,0:T(8,128)}) custom-call(s32[8,128]{1,0:T(8,128)} %broadcast_in_dim.28.slot_mine, bf16[128,8192]{1,0:T(8,128)(2,1)} %acts.1, bf16[128,8192]{1,0:T(8,128)(2,1)} %grads_out.1, f32[64,4096]{1,0:T(8,128)} %bitcast.11, f32[64,4096]{1,0:T(8,128)} %bitcast.12), custom_call_target="tpu_custom_call" | custom-call | tf_op jit(solution)/shard_map/adapter_backward/pallas_call | solution.py:391
  288.2 0.0 copy-start.1
  288.2 0.0 copy-start
  288.2 4.8 %copy.12 = f32[128,8192]{1,0:T(8,128)} copy(f32[128,8192]{1,0:T(8,128)} %get-tuple-element.12) | data formatting | bytes 8388608
  292.9 0.0 copy-done.1
  292.9 1.0 copy.13
  293.9 0.0 copy-done
  293.9 1.0 copy.14
Async XLA Ops:
  288.2 4.8 %copy-start.1 = (f32[64,4096]{1,0:T(8,128)S(1)}, f32[64,4096]{1,0:T(8,128)}, u32[]{:S(2)}) copy-start(f32[64,4096]{1,0:T(8,128)} %get-tuple-element.7) | copy-start | bytes 3145732
  288.2 5.7 %copy-start = (f32[64,4096]{1,0:T(8,128)S(1)}, f32[64,4096]{1,0:T(8,128)}, u32[]{:S(2)}) copy-start(f32[64,4096]{1,0:T(8,128)} %get-tuple-element.8) | copy-start | bytes 3145732

commit v3 on v2

--- a/solution.py
+++ b/solution.py
@@ -124,17 +124,29 @@
     scale,
     coded_in,
     scale_in,
-    acc,
+    ad_out,
+    ad_scale,
+    ad_scale_in,
+    gr_out,
+    gr_scale,
+    gr_in,
+    gr_scale_in,
+    mid,
+    mid_in,
     slot_send,
     slot_recv,
     tok_send,
     tok_recv,
     adapt_send,
     adapt_recv,
+    ad_scale_send,
+    ad_scale_recv,
     part_send,
     part_recv,
     full_send,
     full_recv,
+    mid_send,
+    mid_recv,
     dx_send,
     dx_recv,
     grad_send,
@@ -150,6 +162,11 @@
     tokens = (acts, grads_out)
     halves = (down, up)
     grads = (grad_down, grad_up)
+    inner = size // 2
+    base = (me // inner) * inner
+    spot = me - base
+    across = lax.rem(me + inner, size)
+    quarters = piece // 128
 
     def peer(step):
         return lax.rem(me + step, size)
@@ -159,6 +176,23 @@
 
     def each(body_of):
         lax.fori_loop(1, size, lambda step, carry: (body_of(step), carry)[1], 0)
+
+    def near(step):
+        return lax.rem(spot + step, inner)
+
+    def near_source(step):
+        return lax.rem(spot + inner - step, inner)
+
+    def each_near(body_of):
+        lax.fori_loop(1, inner, lambda step, carry: (body_of(step), carry)[1], 0)
+
+    def code(value):
+        peak = jnp.maximum(jnp.max(jnp.abs(value), axis=0, keepdims=True), 1e-30)
+        whole = jnp.floor(value * (32700.0 / peak) + 0.5).astype(jnp.int32).astype(jnp.int16)
+        return whole, peak * (1.0 / 32700.0)
+
+    def plain(value, unit):
+        return value.astype(jnp.int32).astype(jnp.float32) * unit
 
     def lanes(index, count):
         return pl.ds(pl.multiple_of(index * count, 128), count)
@@ -187,18 +221,27 @@
 
     def adapt_copy(k, dev, at):
         return copy_to(
-            halves[k].at[:, lanes(dev, piece)], adapt_place(k, at),
+            ad_out.at[k, :, lanes(dev, piece)], adapt_place(k, at),
             adapt_send.at[k, dev], adapt_recv.at[k, at], dev,
         )
 
-    def part_copy(k, dev, at):
-        return copy_to(
-            part.at[k, dev], red.at[k, at], part_send.at[k, dev], part_recv.at[k, at], dev
-        )
-
-    def full_copy(k, dev, at, own):
-        return copy_to(
-            full.at[k, own], full.at[k, at], full_send.at[k, dev], full_recv.at[k, at], dev
+    def ad_scale_copy(dev, at):
+        return copy_to(
+            ad_scale.at[dev], ad_scale_in.at[at], ad_scale_send.at[dev], ad_scale_recv.at[at], dev
+        )
+
+    def part_copy(k, side, to, at):
+        return copy_to(
+            part.at[k, to, side], red.at[k, at, side],
+            part_send.at[k, to, side], part_recv.at[k, at, side], base + to,
+        )
+
+    def mid_copy(k):
+        return copy_to(mid.at[k], mid_in.at[k], mid_send.at[k], mid_recv.at[k], across)
+
+    def full_copy(k, to, at):
+        return copy_to(
+            full.at[k, at], full.at[k, at], full_send.at[k, to], full_recv.at[k, at], base + to
         )
 
     def coded_copy(dev, at):
@@ -207,13 +250,15 @@
     def scale_copy(dev, at):
         return copy_to(scale.at[dev], scale_in.at[at], dx_send.at[1, dev], dx_recv.at[1, at], dev)
 
-    def grad_piece(k, dev):
-        return acc.at[k, band(dev // 2, rank), lanes(lax.rem(dev, 2), piece)]
-
     def grad_copy(k, dev, at):
         return copy_to(
-            grad_piece(k, dev), grads[k].at[:, lanes(at, piece)],
-            grad_send.at[k, dev], grad_recv.at[k, at], dev,
+            gr_out.at[k, dev], gr_in.at[k, at], grad_send.at[0, k, dev], grad_recv.at[0, k, at], dev
+        )
+
+    def grad_scale_copy(k, dev, at):
+        return copy_to(
+            gr_scale.at[k, dev], gr_scale_in.at[k, at],
+            grad_send.at[1, k, dev], grad_recv.at[1, k, at], dev,
         )
 
     barrier = pltpu.get_barrier_semaphore()
@@ -223,22 +268,43 @@
 
     each(lambda step: slot_copy(peer(step), me).start())
     own = []
-    for k in (1, 0):
-        each(lambda step: adapt_copy(k, peer(step), me).start())
-
-        def start_tokens(step):
+
+    def start_tokens(k):
+        def one(step):
             for h in range(2):
                 tok_copy(k, h, peer(step), me).start()
 
-        each(start_tokens)
-        own.append(pltpu.make_async_copy(
-            halves[k].at[:, lanes(me, piece)], adapt_place(k, me), local.at[k, 2]))
+        each(one)
         for h in range(2):
-            own.append(pltpu.make_async_copy(
+            copy = pltpu.make_async_copy(
                 tokens[k].at[:, pl.ds(pl.multiple_of(h * half + me * piece, 128), piece)],
-                tok.at[k, band(me, rows), pl.ds(h * piece, piece)], local.at[k, h]))
-    for one in own:
-        one.start()
+                tok.at[k, band(me, rows), pl.ds(h * piece, piece)], local.at[k, h])
+            copy.start()
+            own.append(copy)
+
+    start_tokens(1)
+
+    def code_adapters(dev, carry):
+        for k in range(2):
+            whole, unit = code(halves[k][:, lanes(dev, piece)])
+            ad_out[k, :, lanes(dev, piece)] = whole
+            for q in range(quarters):
+                row = k * quarters + q
+                ad_scale[dev, row:row + 1, :] = unit[:, q * 128:(q + 1) * 128]
+        return carry
+
+    lax.fori_loop(0, size, code_adapters, 0)
+
+    def start_adapters(step):
+        ad_scale_copy(peer(step), me).start()
+        for k in (1, 0):
+            adapt_copy(k, peer(step), me).start()
+
+    each(start_adapters)
+    start_tokens(0)
+    for k in range(2):
+        adapt_place(k, me)[...] = ad_out[k, :, lanes(me, piece)]
+    ad_scale_in[me] = ad_scale[me]
     for one in own:
         one.wait()
     slot_all[me] = slot_mine[...]
@@ -261,38 +327,68 @@
     def project(k):
         each(lambda step: adapt_copy(k, peer(step), source(step)).wait_recv())
         for s in range(slots):
-            high, low = high_low(adapt[k, s * rank:(s + 1) * rank, :])
-            weight[k, s * rank:(s + 1) * rank, :] = high.astype(jnp.bfloat16)
-            weight[k, wide_rank + s * rank:wide_rank + (s + 1) * rank, :] = low.astype(jnp.bfloat16)
-        red[k, me] = partial(k, me)
+            for q in range(2 * quarters):
+                h, p = divmod(q, quarters)
+                span = slice(q * 128, (q + 1) * 128)
+                row = k * quarters + p
+                high, low = high_low(plain(
+                    adapt[k, s * rank:(s + 1) * rank, span], ad_scale_in[2 * s + h, row:row + 1, :]))
+                weight[k, s * rank:(s + 1) * rank, span] = high.astype(jnp.bfloat16)
+                weight[k, wide_rank + s * rank:wide_rank + (s + 1) * rank, span] = low.astype(
+                    jnp.bfloat16)
+        red[k, spot, me // inner] = partial(k, me)
 
         def one(step):
             at = source(step)
             for h in range(2):
                 tok_copy(k, h, peer(step), at).wait_recv()
-            part[k, at] = partial(k, at)
-            part_copy(k, at, me).start()
+            value = partial(k, at)
+            to, side = lax.rem(at, inner), at // inner
+
+            @pl.when(step == inner)
+            def _():
+                red[k, spot, side] = value
+
+            @pl.when(step != inner)
+            def _():
+                part[k, to, side] = value
+                part_copy(k, side, to, spot).start()
 
         each(one)
 
-    def combine(k):
-        each(lambda step: part_copy(k, peer(step), source(step)).wait_recv())
-        full[k, me] = jnp.sum(red[k], axis=0)
-        each(lambda step: full_copy(k, peer(step), me, me).start())
+    def meet(k):
+        def one(step):
+            for side in range(2):
+                part_copy(k, side, near(step), near_source(step)).wait_recv()
+
+        each_near(one)
+        mid[k] = jnp.sum(red[k], axis=0)
+        mid_copy(k).start()
+
+    def tell(k):
+        mid_copy(k).wait_recv()
+        full[k, spot] = mid[k] + mid_in[k]
+        each_near(lambda step: full_copy(k, near(step), spot).start())
+
+    def hear(k):
+        each_near(lambda step: full_copy(k, near(step), near_source(step)).wait_recv())
 
     def expand(k, at):
         ids = slot_all[at][0:1, :]
-        high, low = high_low(full[k, at])
+        high, low = high_low(full[k, lax.rem(at, inner), at // inner])
         for s in range(slots):
             spread[k, s * rank:(s + 1) * rank, lanes(at, rows)] = jnp.where(
                 ids == s, high, 0.0).astype(jnp.bfloat16)
             spread[k, wide_rank + s * rank:wide_rank + (s + 1) * rank, lanes(at, rows)] = jnp.where(
                 ids == s, low, 0.0).astype(jnp.bfloat16)
 
+    each(lambda step: ad_scale_copy(peer(step), source(step)).wait_recv())
     project(1)
-    combine(1)
+    meet(1)
+    tell(1)
     project(0)
-    combine(0)
+    meet(0)
+    hear(1)
 
     def rows_grad(at, into, into_scale, dev):
         expand(1, at)
@@ -301,10 +397,7 @@
         dx = mm(high, weight[0, :wide_rank, :], ((0,), (0,)))
         dx = dx + mm(low, weight[0, :wide_rank, :], ((0,), (0,)))
         dx = 2.0 * (dx + mm(high, weight[0, wide_rank:, :], ((0,), (0,))))
-        peak = jnp.maximum(jnp.max(jnp.abs(dx), axis=0, keepdims=True), 1e-30)
-        value = jnp.floor(dx * (32700.0 / peak) + 0.5)
-        into[dev] = value.astype(jnp.int32).astype(jnp.int16)
-        unit = peak * (1.0 / 32700.0)
+        into[dev], unit = code(dx)
         for q in range(2 * piece // 128):
             into_scale[dev, q:q + 1, :] = unit[:, q * 128:(q + 1) * 128]
 
@@ -312,7 +405,6 @@
 
     def send_rows(step):
         at = source(step)
-        full_copy(1, peer(step), at, me).wait_recv()
         rows_grad(at, coded, scale, at)
         coded_copy(at, me).start()
         scale_copy(at, me).start()
@@ -322,30 +414,43 @@
     def weight_grad(k):
         def column(h, carry):
             value = mm(spread[1 - k], tok[k, :, lanes(h, piece)], ((1,), (0,)))
-            acc[k, :, lanes(h, piece)] = 2.0 * (value[:wide_rank] + value[wide_rank:])
+            value = 2.0 * (value[:wide_rank] + value[wide_rank:])
+            for s in range(slots):
+                whole, unit = code(value[s * rank:(s + 1) * rank])
+                gr_out[k, 2 * s + h] = whole
+                for q in range(quarters):
+                    gr_scale[k, 2 * s + h, q:q + 1, :] = unit[:, q * 128:(q + 1) * 128]
             return carry
 
         lax.fori_loop(0, 2, column, 0)
-        grads[k][:, lanes(me, piece)] = grad_piece(k, me)[...]
-        each(lambda step: grad_copy(k, peer(step), me).start())
+        gr_in[k, me] = gr_out[k, me]
+        gr_scale_in[k, me] = gr_scale[k, me]
+
+        def send(step):
+            grad_copy(k, peer(step), me).start()
+            grad_scale_copy(k, peer(step), me).start()
+
+        each(send)
 
     weight_grad(0)
+    tell(0)
+    hear(0)
     expand(0, me)
-
-    def low_rows(step):
-        at = source(step)
-        full_copy(0, peer(step), at, me).wait_recv()
-        expand(0, at)
-
-    each(low_rows)
+    each(lambda step: expand(0, source(step)))
     weight_grad(1)
+
+    def decode_grad(k, at):
+        for q in range(quarters):
+            start = pl.multiple_of(at * piece + q * 128, 128)
+            grads[k][:, pl.ds(start, 128)] = plain(
+                gr_in[k, at, :, q * 128:(q + 1) * 128], gr_scale_in[k, at, q:q + 1, :])
 
     def decode(at):
         for q in range(2 * piece // 128):
             h, r = divmod(q * 128, piece)
-            value = coded_in[at, :, q * 128:(q + 1) * 128].astype(jnp.int32).astype(jnp.float32)
+            value = coded_in[at, :, q * 128:(q + 1) * 128]
             start = pl.multiple_of(h * half + at * piece + r, 128)
-            input_grad[:, pl.ds(start, 128)] = value * scale_in[at, q:q + 1, :]
+            input_grad[:, pl.ds(start, 128)] = plain(value, scale_in[at, q:q + 1, :])
 
     decode(me)
 
@@ -357,21 +462,44 @@
 
     each(take)
 
+    def take_grad(k):
+        decode_grad(k, me)
+
+        def one(step):
+            at = source(step)
+            grad_copy(k, peer(step), at).wait_recv()
+            grad_scale_copy(k, peer(step), at).wait_recv()
+            decode_grad(k, at)
+
+        each(one)
+
+    take_grad(0)
+    take_grad(1)
+
     def finish(step):
-        dev, at = peer(step), source(step)
+        dev = peer(step)
         for k in range(2):
-            grad_copy(k, dev, at).wait_recv()
             grad_copy(k, dev, me).wait_send()
+            grad_scale_copy(k, dev, me).wait_send()
             for h in range(2):
                 tok_copy(k, h, dev, me).wait_send()
             adapt_copy(k, dev, me).wait_send()
-            part_copy(k, dev, me).wait_send()
-            full_copy(k, dev, me, me).wait_send()
         slot_copy(dev, me).wait_send()
+        ad_scale_copy(dev, me).wait_send()
         coded_copy(dev, me).wait_send()
         scale_copy(dev, me).wait_send()
 
     each(finish)
+
+    def finish_near(step):
+        for k in range(2):
+            for side in range(2):
+                part_copy(k, side, near(step), spot).wait_send()
+            full_copy(k, near(step), spot).wait_send()
+
+    each_near(finish_near)
+    for k in range(2):
+        mid_copy(k).wait_send()
 
 
 def by_columns(acts, grads_out, tenant_ids, owner, a_half, b_half):
@@ -395,30 +523,40 @@
             jax.ShapeDtypeStruct((rank, width // 2), f32),
             jax.ShapeDtypeStruct((rank, width // 2), f32),
         ),
-        in_specs=[vmem, hbm, hbm, hbm, hbm],
+        in_specs=[vmem, hbm, hbm, vmem, vmem],
         out_specs=(vmem, vmem, vmem),
         scratch_shapes=[
             pltpu.VMEM((size, 8, rows), jnp.int32),
             pltpu.VMEM((2, total, chunk), bf16),
-            pltpu.VMEM((2, slots * rank, chunk), f32),
+            pltpu.VMEM((2, slots * rank, chunk), jnp.int16),
             pltpu.VMEM((2, 2 * slots * rank, chunk), bf16),
             pltpu.VMEM((2, 2 * slots * rank, total), bf16),
-            pltpu.VMEM((2, size, rank, rows), f32),
-            pltpu.VMEM((2, size, rank, rows), f32),
-            pltpu.VMEM((2, size, rank, rows), f32),
+            pltpu.VMEM((2, size // 2, 2, rank, rows), f32),
+            pltpu.VMEM((2, size // 2, 2, rank, rows), f32),
+            pltpu.VMEM((2, size // 2, 2, rank, rows), f32),
             pltpu.VMEM((size, rows, chunk), jnp.int16),
             pltpu.VMEM((size, 8, 128), f32),
             pltpu.VMEM((size, rows, chunk), jnp.int16),
             pltpu.VMEM((size, 8, 128), f32),
-            pltpu.VMEM((2, slots * rank, chunk), f32),
+            pltpu.VMEM((2, rank, width // 2), jnp.int16),
+            pltpu.VMEM((size, 8, 128), f32),
+            pltpu.VMEM((size, 8, 128), f32),
+            pltpu.VMEM((2, size, rank, chunk // 2), jnp.int16),
+            pltpu.VMEM((2, size, 8, 128), f32),
+            pltpu.VMEM((2, size, rank, chunk // 2), jnp.int16),
+            pltpu.VMEM((2, size, 8, 128), f32),
+            pltpu.VMEM((2, 2, rank, rows), f32),
+            pltpu.VMEM((2, 2, rank, rows), f32),
             dma((size,)), dma((size,)),
             dma((2, size, 2)), dma((2, size, 2)),
             dma((2, size)), dma((2, size)),
+            dma((size,)), dma((size,)),
+            dma((2, size // 2, 2)), dma((2, size // 2, 2)),
+            dma((2, size // 2)), dma((2, size // 2)),
+            dma((2,)), dma((2,)),
             dma((2, size)), dma((2, size)),
-            dma((2, size)), dma((2, size)),
-            dma((2, size)), dma((2, size)),
-            dma((2, size)), dma((2, size)),
-            dma((2, 3)),
+            dma((2, 2, size)), dma((2, 2, size)),
+            dma((2, 2)),
         ],
         compiler_params=pltpu.CompilerParams(
             collective_id=0, has_side_effects=True, vmem_limit_bytes=56 * 2**20

time: 295 us -> 233 us (0.79)
  Pallas kernels: 286 us -> 222 us
    pallas_call x1, Pallas kernels: 286 us -> 222 us  [by_columns(): pl.pallas_call(functools.partial(kernel, size, slots), out_shape=(jax.Sha...]
where the time goes in v3:
time: 233 us; the launch traced here: 230 us
  Pallas kernels  222 us (95%)
  local copies, waits for them, and re-layouts  7.3 us (3%)
    pallas_call x1, Pallas kernels, by_columns(): pl.pallas_call(functools.partial(kernel, size, slots), out_shape=(jax.Sha...  222 us
    unnamed x7, local copies, waits for them, and re-layouts  6.7 us

profile of v3, /device:TPU:13, one launch (start us, length us, event | category | flops | bytes accessed | tf_op | source)
XLA Modules:
  0.0 230.4 jit_solution(15277196362239042843)
XLA Ops:
  0.6 0.8 select_reduce_fusion
  1.4 0.6 broadcast_in_dim.28.slot_mine
  2.0 221.7 %adapter_backward.1 = (f32[128,8192]{1,0:T(8,128)}, f32[64,4096]{1,0:T(8,128)}, f32[64,4096]{1,0:T(8,128)}) custom-call(s32[8,128]{1,0:T(8,128)} %broadcast_in_dim.28.slot_mine, bf16[128,8192]{1,0:T(8,128)(2,1)} %acts.1, bf16[128,8192]{1,0:T(8,128)(2,1)} %grads_out.1, f32[64,4096]{1,0:T(8,128)} %bitcast.11, f32[64,4096]{1,0:T(8,128)} %bitcast.12), custom_call_target="tpu_custom_call" | custom-call | tf_op jit(solution)/shard_map/adapter_backward/pallas_call | solution.py:519
  223.7 0.0 copy-start.1
  223.7 0.0 copy-start
  223.7 4.8 %copy.12 = f32[128,8192]{1,0:T(8,128)} copy(f32[128,8192]{1,0:T(8,128)} %get-tuple-element.12) | data formatting | bytes 8388608
  228.4 0.0 copy-done.1
  228.4 1.0 copy.13
  229.4 0.0 copy-done
  229.4 1.0 copy.14
Async XLA Ops:
  223.7 4.8 %copy-start.1 = (f32[64,4096]{1,0:T(8,128)S(1)}, f32[64,4096]{1,0:T(8,128)}, u32[]{:S(2)}) copy-start(f32[64,4096]{1,0:T(8,128)} %get-tuple-element.7) | copy-start | bytes 3145732
  223.7 5.7 %copy-start = (f32[64,4096]{1,0:T(8,128)S(1)}, f32[64,4096]{1,0:T(8,128)}, u32[]{:S(2)}) copy-start(f32[64,4096]{1,0:T(8,128)} %get-tuple-element.8) | copy-start | bytes 3145732

commit v4 on v3

--- a/solution.py
+++ b/solution.py
@@ -109,7 +109,8 @@
     grads_out,
     down,
     up,
-    input_grad,
+    coded_in,
+    scale_in,
     grad_down,
     grad_up,
     slot_all,
@@ -122,8 +123,6 @@
     full,
     coded,
     scale,
-    coded_in,
-    scale_in,
     ad_out,
     ad_scale,
     ad_scale_in,
@@ -445,20 +444,11 @@
             grads[k][:, pl.ds(start, 128)] = plain(
                 gr_in[k, at, :, q * 128:(q + 1) * 128], gr_scale_in[k, at, q:q + 1, :])
 
-    def decode(at):
-        for q in range(2 * piece // 128):
-            h, r = divmod(q * 128, piece)
-            value = coded_in[at, :, q * 128:(q + 1) * 128]
-            start = pl.multiple_of(h * half + at * piece + r, 128)
-            input_grad[:, pl.ds(start, 128)] = plain(value, scale_in[at, q:q + 1, :])
-
-    decode(me)
 
     def take(step):
         at = source(step)
         coded_copy(peer(step), at).wait_recv()
         scale_copy(peer(step), at).wait_recv()
-        decode(at)
 
     each(take)
 
@@ -516,15 +506,16 @@
     hbm = pl.BlockSpec(memory_space=pl.ANY)
     dma = pltpu.SemaphoreType.DMA
     f32, bf16 = jnp.float32, jnp.bfloat16
-    input_grad, grad_down, grad_up = pl.pallas_call(
+    coded, scale, grad_down, grad_up = pl.pallas_call(
         functools.partial(kernel, size, slots),
         out_shape=(
-            jax.ShapeDtypeStruct((rows, width), f32),
+            jax.ShapeDtypeStruct((size, rows, chunk), jnp.int16),
+            jax.ShapeDtypeStruct((size, 8, 128), f32),
             jax.ShapeDtypeStruct((rank, width // 2), f32),
             jax.ShapeDtypeStruct((rank, width // 2), f32),
         ),
         in_specs=[vmem, hbm, hbm, vmem, vmem],
-        out_specs=(vmem, vmem, vmem),
+        out_specs=(vmem, vmem, vmem, vmem),
         scratch_shapes=[
             pltpu.VMEM((size, 8, rows), jnp.int32),
             pltpu.VMEM((2, total, chunk), bf16),
@@ -534,8 +525,6 @@
             pltpu.VMEM((2, size // 2, 2, rank, rows), f32),
             pltpu.VMEM((2, size // 2, 2, rank, rows), f32),
             pltpu.VMEM((2, size // 2, 2, rank, rows), f32),
-            pltpu.VMEM((size, rows, chunk), jnp.int16),
-            pltpu.VMEM((size, 8, 128), f32),
             pltpu.VMEM((size, rows, chunk), jnp.int16),
             pltpu.VMEM((size, 8, 128), f32),
             pltpu.VMEM((2, rank, width // 2), jnp.int16),
@@ -563,6 +552,10 @@
         ),
         name="adapter_backward",
     )(slot_mine, acts, grads_out, a_half[0].T, b_half[0])
+    unit = scale[:, :chunk // 128].reshape(size, 1, chunk)
+    input_grad = coded.astype(f32) * unit
+    input_grad = input_grad.reshape(size, rows, 2, chunk // 2).transpose(1, 2, 0, 3)
+    input_grad = input_grad.reshape(rows, width)
     return input_grad, grad_down.T[None], grad_up[None]
 
 

time: 233 us -> 249 us (1.069)
  local copies, waits for them, and re-layouts: 7.3 us -> 19.2 us
  other arithmetic: 0.76 us -> 5.08 us
    reshape x0 -> x1, local copies, waits for them, and re-layouts: none -> 5.87 us  [by_columns(): input_grad.reshape(size, rows, 2, chunk // 2).transpose(1, 2, 0, 3)]
    transpose x0 -> x1, local copies, waits for them, and re-layouts: none -> 4.62 us  [by_columns(): input_grad.reshape(size, rows, 2, chunk // 2).transpose(1, 2, 0, 3)]
    mul x0 -> x1, other arithmetic: none -> 4.33 us  [by_columns(): input_grad = coded.astype(f32) * unit]
    unnamed x7 -> x8, local copies, waits for them, and re-layouts: 6.7 us -> 7.29 us
where the time goes in v4:
time: 249 us; the launch traced here: 246 us
  Pallas kernels  221 us (89%)
  local copies, waits for them, and re-layouts  19.2 us (8%)
  other arithmetic  5.08 us (2%)
    pallas_call x1, Pallas kernels, by_columns(): pl.pallas_call(functools.partial(kernel, size, slots), out_shape=(jax.Sha...  221 us
    unnamed x8, local copies, waits for them, and re-layouts  7.29 us
    reshape x1, local copies, waits for them, and re-layouts, by_columns(): input_grad.reshape(size, rows, 2, chunk // 2).transpose(1, 2, 0, 3)  5.87 us

profile of v4, /device:TPU:13, one launch (start us, length us, event | category | flops | bytes accessed | tf_op | source)
XLA Modules:
  0.0 246.0 jit_solution(16226345101332245822)
XLA Ops:
  0.6 0.8 select_reduce_fusion
  1.4 0.6 broadcast_in_dim.28.slot_mine
  2.0 221.1 %adapter_backward.1 = (s16[16,128,512]{2,1,0:T(8,128)(2,1)}, f32[16,8,128]{2,1,0:T(8,128)}, f32[64,4096]{1,0:T(8,128)}, f32[64,4096]{1,0:T(8,128)}) custom-call(s32[8,128]{1,0:T(8,128)} %broadcast_in_dim.28.slot_mine, bf16[128,8192]{1,0:T(8,128)(2,1)} %acts.1, bf16[128,8192]{1,0:T(8,128)(2,1)} %grads_out.1, f32[64,4096]{1,0:T(8,128)} %bitcast.22, ...), custom_call_target="tpu_custom_call" | custom-call | tf_op jit(solution)/shard_map/adapter_backward/pallas_call | solution.py:509
  223.0 0.8 slice.3
  223.9 4.3 %convert_multiply_fusion = f32[16,128,512]{2,1,0:T(8,128)} fusion(s16[16,128,512]{2,1,0:T(8,128)(2,1)} %get-tuple-element.7, f32[16,512]{1,0:T(8,128)S(1)} %bitcast.24), kind=kLoop, calls=%fused_computation | loop fusion | flops 2097152 | bytes 6324224 | tf_op jit(solution)/shard_map/mul | solution.py:556
  228.2 5.9 %reshape.16 = f32[16,128,2,256]{3,2,1,0:T(2,128)} reshape(f32[16,128,512]{2,1,0:T(8,128)} %convert_multiply_fusion) | data formatting | bytes 8388608 | tf_op jit(solution)/shard_map/reshape | solution.py:557
  234.1 4.6 %copy.10 = f32[128,2,16,256]{3,2,1,0:T(8,128)S(1)} copy(f32[128,2,16,256]{3,1,0,2:T(2,128)} %bitcast.17) | data formatting | bytes 8388608 | tf_op jit(solution)/shard_map/transpose | solution.py:557
  238.7 0.0 copy-start.1
  238.7 0.0 copy-start
  238.7 5.3 %copy.12 = f32[16,8,32,256]{3,1,2,0:T(8,128)} copy(f32[16,8,32,256]{3,2,1,0:T(8,128)S(1)} %bitcast.18) | data formatting | bytes 8388608
  244.1 0.0 copy-done.1
  244.1 1.0 copy.17
  245.0 0.0 copy-done
  245.0 1.0 copy.18
  (1 shorter events, 0.0 us)
Async XLA Ops:
  238.7 5.4 %copy-start.1 = (f32[64,4096]{1,0:T(8,128)S(1)}, f32[64,4096]{1,0:T(8,128)}, u32[]{:S(2)}) copy-start(f32[64,4096]{1,0:T(8,128)} %get-tuple-element.9) | copy-start | bytes 3145732
  238.7 6.3 %copy-start = (f32[64,4096]{1,0:T(8,128)S(1)}, f32[64,4096]{1,0:T(8,128)}, u32[]{:S(2)}) copy-start(f32[64,4096]{1,0:T(8,128)} %get-tuple-element.10) | copy-start | bytes 3145732
